TPU v7x, 512 devices: a whole 4x4x16 slice. The times are simulated.
512 devices in a mesh: wide: 128 (over z, x, core), narrow: 4 (over y).
Axes of the slice: x: 4, y: 4, z: 16, core: 2. Of those that a mesh axis runs over, the one named last changes fastest.
Arguments:
- position: float32 [3, 524288], P(None, ('wide', 'narrow')), may hold values from -6 to 6
- velocity: float32 [3, 524288], P(None, ('wide', 'narrow')), may hold values from -6 to 6
- mass: float32 [524288], P(('wide', 'narrow')), may hold values from 0.5 to 2
- energy: float32 [524288], P(('wide', 'narrow')), may hold values from 0.5 to 2
- smoothing: float32 [524288], P(('wide', 'narrow')), may hold values from 1.5 to 3
- local_near: int32 [4096], P(('wide', 'narrow')), may hold values from 0 to 7
- dens_block: int32 [4096], P(('wide', 'narrow')), may hold values from 0 to 7
- dens_dest: int32 [4096, 1], P(('wide', 'narrow')), may hold values from 0 to 3; in each aligned block of 8 rows (0 to 7, 8 to 15, ...) at most 6 rows name the same one
- dens_near: int32 [4096, 2], P(('wide', 'narrow')), may hold values from 0 to 7
- force_block: int32 [65536], P(('wide', 'narrow')), may hold values from 0 to 7
- force_dest: int32 [65536, 1], P(('wide', 'narrow')), may hold values from 0 to 127; in each aligned block of 128 rows (0 to 127, 128 to 255, ...) at most 3 rows name the same one
- force_near: int32 [65536, 2], P(('wide', 'narrow')), may hold values from 0 to 7
Outputs:
- density: float32 [524288], P(('wide', 'narrow'))
- accel: float32 [3, 524288], P(None, ('wide', 'narrow'))
- energy_rate: float32 [524288], P(('wide', 'narrow'))
Inputs may be any that keep to these rules, and one draw needn't show every extreme that they name: `dens_dest`: among the 8 rows of one device no narrow index is named by more than 6 rows; some index is named exactly 6 times by the rows of some device. `force_dest`: among the 128 rows of one device no wide index is named by more than 3 rows; some index is named exactly 3 times by the rows of some device.
All inputs are finite; a program needn't handle non-finite values.
Results may differ from a plain program's by a relative error of at most 0.0003.
Values sent between devices are 32-bit elements; how exact they have to be, the bound alone decides.
A program may use at most 64 MiB of HBM per device.

v0:
```python
import math

import jax
import jax.numpy as jnp
from jax import lax
from jax.sharding import PartitionSpec as P

PASSES = 3


kernel_norm = math.pi ** (-1.5)
target_count = 24.0
gamma_gas = 5.0 / 3.0


def density_tile(target, source):
    dist_sq = jnp.zeros((target.shape[0], target.shape[2], source.shape[2]), target.dtype)
    for comp in range(3):
        delta = target[:, comp, :, None] - source[:, comp, None, :]
        dist_sq = dist_sq + delta * delta
    width = target[:, 3, :, None]
    weight = jnp.exp(-dist_sq / (width * width)) * source[:, 3, None, :]
    return jnp.stack([jnp.sum(weight, -1), jnp.sum(weight * dist_sq, -1)], axis=1)


def force_tile(target, source):
    deltas = [target[:, comp, :, None] - source[:, comp, None, :] for comp in range(3)]
    dist_sq = deltas[0] * deltas[0] + deltas[1] * deltas[1] + deltas[2] * deltas[2]
    vdot = (target[:, 3, :, None] - source[:, 3, None, :]) * deltas[0]
    vdot = vdot + (target[:, 4, :, None] - source[:, 4, None, :]) * deltas[1]
    vdot = vdot + (target[:, 5, :, None] - source[:, 5, None, :]) * deltas[2]
    width_i = target[:, 6, :, None]
    width_j = source[:, 7, None, :]
    grad_i = 2.0 * kernel_norm * jnp.exp(-dist_sq / (width_i * width_i)) / width_i**5
    grad_j = 2.0 * kernel_norm * jnp.exp(-dist_sq / (width_j * width_j)) / width_j**5
    mean_width = 0.5 * (width_i + width_j)
    approach = jnp.minimum(mean_width * vdot / (dist_sq + 0.01 * mean_width * mean_width), 0.0)
    sound_mean = 0.5 * (target[:, 9, :, None] + source[:, 10, None, :])
    rho_mean = 0.5 * (target[:, 7, :, None] + source[:, 8, None, :])
    visc = (-sound_mean * approach + 2.0 * approach * approach) / rho_mean
    grad_mean = 0.5 * (grad_i + grad_j)
    mass_j = source[:, 6, None, :]
    own_term = target[:, 8, :, None] * grad_i
    push = mass_j * (own_term + source[:, 9, None, :] * grad_j + visc * grad_mean)
    heat = -mass_j * (own_term + 0.5 * visc * grad_mean) * vdot
    return jnp.stack(
        [
            jnp.sum(push * deltas[0], -1),
            jnp.sum(push * deltas[1], -1),
            jnp.sum(push * deltas[2], -1),
            jnp.sum(heat, -1),
        ],
        axis=1,
    )


def grouped(kernel, target, source):
    items = target.shape[0]
    group = max((size for size in range(1, 17) if items % size == 0))
    if group == items:
        return kernel(target, source)
    shaped_t = target.reshape((items // group, group) + target.shape[1:])
    shaped_s = source.reshape((items // group, group) + source.shape[1:])
    result = lax.map(lambda pair: kernel(pair[0], pair[1]), (shaped_t, shaped_s))
    return result.reshape((items,) + result.shape[2:])


def join_blocks(picked):
    return picked.transpose(0, 2, 1, 3).reshape(
        picked.shape[0], picked.shape[2], picked.shape[1] * picked.shape[3]
    )


def dispatch(dest, peers, capacity):
    entries = dest.shape[0]
    named = dest[:, 0]
    onehot = (named[:, None] == jnp.arange(peers, dtype=jnp.int32)[None, :]).astype(jnp.int32)
    before = jnp.cumsum(onehot, axis=0) - onehot
    place = jnp.sum(before * onehot, axis=1)
    slot_of = named * capacity + place
    table = (slot_of[None, :] == jnp.arange(peers * capacity, dtype=jnp.int32)[:, None]).astype(
        jnp.int32
    )
    slot_entry = jnp.dot(
        table, jnp.arange(entries, dtype=jnp.int32), preferred_element_type=jnp.int32
    )
    filled = jnp.sum(table, axis=1)
    return (slot_of, slot_entry, filled)


def add_exports(local_part, rows, remote_part, count):
    onehot = (jnp.arange(count, dtype=jnp.int32)[:, None] == rows[None, :]).astype(jnp.float32)
    added = jnp.dot(
        onehot, remote_part.reshape(remote_part.shape[0], -1), precision=lax.Precision.HIGHEST
    )
    return local_part + added.reshape(local_part.shape)


def on_device(
    position,
    velocity,
    mass,
    energy,
    smoothing,
    local_near,
    dens_block,
    dens_dest,
    dens_near,
    force_block,
    force_dest,
    force_near,
):
    count = local_near.shape[0]
    block_size = position.shape[1] // count

    def blocks_of(field):
        return field.reshape(field.shape[0], count, block_size).transpose(1, 0, 2)

    pos_blocks = blocks_of(position)
    vel_blocks = blocks_of(velocity)
    mass_blocks = blocks_of(mass[None])
    energy_blocks = blocks_of(energy[None])
    width = blocks_of(smoothing[None])
    narrow_peers = lax.axis_size("narrow")
    wide_peers = lax.axis_size("wide")
    dens_cap = max(2, (3 * dens_block.shape[0] + narrow_peers - 1) // narrow_peers)
    force_cap = max(2, (3 * force_block.shape[0] + wide_peers - 1) // wide_peers)
    dens_slot_of, dens_entry, dens_filled = dispatch(dens_dest, narrow_peers, dens_cap)
    dens_source = jnp.concatenate([pos_blocks, mass_blocks], axis=1)
    dens_local_src = join_blocks(jnp.stack([dens_source, dens_source[local_near]], axis=1))
    dens_wanted = lax.all_to_all(
        dens_near[dens_entry], "narrow", split_axis=0, concat_axis=0, tiled=True
    )
    dens_served = join_blocks(dens_source[dens_wanted])
    dens_pad = jnp.array([0.0, 0.0, 0.0, 1.0], jnp.float32)[None, :, None]
    total = width
    for step in range(PASSES):
        targets = jnp.concatenate([pos_blocks, width], axis=1)
        local_part = grouped(density_tile, targets, dens_local_src)
        sent = jnp.where(dens_filled[:, None, None] > 0, targets[dens_block[dens_entry]], dens_pad)
        answer_partial_value = grouped(
            density_tile,
            lax.all_to_all(sent, "narrow", split_axis=0, concat_axis=0, tiled=True),
            dens_served,
        )
        returned = lax.all_to_all(
            answer_partial_value, "narrow", split_axis=0, concat_axis=0, tiled=True
        )
        remote_part = returned[dens_slot_of]
        sums = add_exports(local_part, dens_block, remote_part, count)
        total = sums[:, 0:1]
        moment = sums[:, 1:2]
        if step + 1 < PASSES:
            ratio = jnp.log(kernel_norm * total / (target_count * mass_blocks))
            slope = 2.0 * moment / (width * width * total)
            width = width * jnp.exp(-ratio / (3.0 + slope))
    rho = kernel_norm * total / width**3
    press_coef = (gamma_gas - 1.0) * energy_blocks / rho
    sound = jnp.sqrt(gamma_gas * (gamma_gas - 1.0) * energy_blocks)
    force_target = jnp.concatenate([pos_blocks, vel_blocks, width, rho, press_coef, sound], axis=1)
    force_source = jnp.concatenate(
        [pos_blocks, vel_blocks, mass_blocks, width, rho, press_coef, sound], axis=1
    )
    force_local_src = join_blocks(jnp.stack([force_source, force_source[local_near]], axis=1))
    local_force = grouped(force_tile, force_target, force_local_src)
    force_slot_of, force_entry, force_filled = dispatch(force_dest, wide_peers, force_cap)
    force_wanted = lax.all_to_all(
        force_near[force_entry], "wide", split_axis=0, concat_axis=0, tiled=True
    )
    force_served = join_blocks(force_source[force_wanted])
    force_pad = jnp.array([0.0, 0.0, 0.0, 0.0, 0.0, 0.0, 1.0, 1.0, 0.0, 0.0], jnp.float32)[
        None, :, None
    ]
    sent_state = jnp.where(
        force_filled[:, None, None] > 0, force_target[force_block[force_entry]], force_pad
    )
    partial_value = grouped(
        force_tile,
        lax.all_to_all(sent_state, "wide", split_axis=0, concat_axis=0, tiled=True),
        force_served,
    )
    returned_force = lax.all_to_all(partial_value, "wide", split_axis=0, concat_axis=0, tiled=True)
    remote_force = returned_force[force_slot_of]
    result = add_exports(local_force, force_block, remote_force, count)
    accel = result[:, 0:3].transpose(1, 0, 2).reshape(3, count * block_size)
    energy_rate = result[:, 3].reshape(count * block_size)
    return (rho.reshape(count * block_size), accel, energy_rate)


def solution(mesh):
    in_specs = (
        P(None, ("wide", "narrow")),
        P(None, ("wide", "narrow")),
        P(("wide", "narrow")),
        P(("wide", "narrow")),
        P(("wide", "narrow")),
        P(("wide", "narrow")),
        P(("wide", "narrow")),
        P(("wide", "narrow"), None),
        P(("wide", "narrow"), None),
        P(("wide", "narrow")),
        P(("wide", "narrow"), None),
        P(("wide", "narrow"), None),
    )
    out_specs = (P(("wide", "narrow")), P(None, ("wide", "narrow")), P(("wide", "narrow")))
    return jax.shard_map(
        on_device, mesh=mesh, in_specs=in_specs, out_specs=out_specs, check_vma=False
    )
```

profile of v0, /device:TPU:1, one launch (start us, length us, event | category | flops | bytes accessed | tf_op | source)
XLA Modules:
  0.0 697.7 jit_solution(14259564517175307544)
XLA Ops:
  89.3 27.0 %all-to-all-start.7 = ((s32[128,3,2]{1,2,0:T(2,128)}), s32[128,3,2]{1,2,0:T(2,128)S(1)}, u32[]{:S(2)}, u32[]{:S(2)}) async-start(s32[128,3,2]{1,2,0:T(2,128)} %copy.162), calls=%async_computation.7 | async-start | bytes 262144 | tf_op jit(solution)/shard_map/all_to_all | solution.py:167
  121.8 10.6 %all-to-all-done.7 = s32[128,3,2]{1,2,0:T(2,128)S(1)} async-done(((s32[128,3,2]{1,2,0:T(2,128)}), s32[128,3,2]{1,2,0:T(2,128)S(1)}, u32[]{:S(2)}, u32[]{:S(2)}) %all-to-all-start.7) | async-done | bytes 3104 | tf_op jit(solution)/shard_map/all_to_all | solution.py:167
  132.4 7.2 %all-to-all-start.8 = ((f32[384,10,128]{2,1,0:T(8,128)}), f32[384,10,128]{2,1,0:T(8,128)S(1)}, u32[]{:S(2)}, u32[]{:S(2)}) async-start(f32[384,10,128]{2,1,0:T(8,128)} %broadcast_select_fusion), calls=%async_computation.8 | async-start | bytes 6291456 | tf_op jit(solution)/shard_map/all_to_all | solution.py:179
  152.0 6.5 reshape_reshape.9
  158.5 121.7 %all-to-all-done.8 = f32[384,10,128]{2,1,0:T(8,128)S(1)} async-done(((f32[384,10,128]{2,1,0:T(8,128)}), f32[384,10,128]{2,1,0:T(8,128)S(1)}, u32[]{:S(2)}, u32[]{:S(2)}) %all-to-all-start.8) | async-done | bytes 1966112 | tf_op jit(solution)/shard_map/all_to_all | solution.py:179
  282.3 357.7 %while.45 = (s32[]{:T(128)}, f32[24,16,4,128]{3,1,0,2:T(8,128)}, f32[24,16,11,256]{3,1,0,2:T(8,128)}, f32[24,16,10,128]{3,1,2,0:T(8,128)}, s32[]{:T(128)}) while((s32[]{:T(128)}, f32[24,16,4,128]{3,1,0,2:T(8,128)}, f32[24,16,11,256]{3,1,0,2:T(8,128)}, f32[24,16,10,128]{3,1,2,0:T(8,128)}, s32[]{:T(128)}) %tuple.194), condition=%wide.region_33.34_spmd, body=%wide.region_28.33_spmd.sunk | while | flops 54040576 | bytes 1827397 | solution.py:64
  284.1 6.4 fusion.86
  299.0 6.4 fusion.86
  313.9 6.4 fusion.86
  328.8 6.4 fusion.86
  343.7 6.4 fusion.86
  358.7 6.4 fusion.86
  373.5 6.4 fusion.86
  388.4 6.4 fusion.86
  403.4 6.4 fusion.86
  418.3 6.4 fusion.86
  433.2 6.4 fusion.86
  448.1 6.4 fusion.86
  463.0 6.4 fusion.86
  537.5 6.4 fusion.86
  582.2 6.4 fusion.86
  612.0 6.4 fusion.86
  642.5 11.4 %all-to-all-start.9 = ((f32[384,4,128]{2,1,0:T(4,128)}), f32[384,4,128]{2,1,0:T(4,128)S(1)}, u32[]{:S(2)}, u32[]{:S(2)}) async-start(f32[384,4,128]{2,1,0:T(4,128)} %copy.172), calls=%async_computation.9 | async-start | bytes 1572864 | tf_op jit(solution)/shard_map/all_to_all | solution.py:182
  660.9 34.4 %all-to-all-done.9 = f32[384,4,128]{2,1,0:T(4,128)S(1)} async-done(((f32[384,4,128]{2,1,0:T(4,128)}), f32[384,4,128]{2,1,0:T(4,128)S(1)}, u32[]{:S(2)}, u32[]{:S(2)}) %all-to-all-start.9) | async-done | bytes 786464 | tf_op jit(solution)/shard_map/all_to_all | solution.py:182
  (376 shorter events, 388.8 us)
Async XLA Ops:
  5.1 17.4 %all-to-all-start.1 = ((s32[4,6,2]{1,2,0:T(2,128)}), s32[4,6,2]{1,2,0:T(2,128)S(1)}, u32[]{:S(2)}, u32[]{:S(2)}) async-start(s32[4,6,2]{1,2,0:T(2,128)} %copy.139), calls=%async_computation.1 | async-start | bytes 8192 | tf_op jit(solution)/shard_map/all_to_all | solution.py:131
  22.5 8.6 %all-to-all-start = ((f32[24,4,128]{2,1,0:T(4,128)}), f32[24,4,128]{2,1,0:T(4,128)S(1)}, u32[]{:S(2)}, u32[]{:S(2)}) async-start(f32[24,4,128]{2,1,0:T(4,128)} %broadcast_select_fusion.3), calls=%async_computation | async-start | bytes 98304 | tf_op jit(solution)/shard_map/all_to_all | solution.py:143
  31.7 8.1 %copy-start = (s32[128]{0:T(128)S(1)}, s32[128]{0:T(128)}, u32[]{:S(2)}) copy-start(s32[128]{0:T(128)} %param.31) | copy-start | bytes 1540
  36.4 8.2 %copy-start.1 = (s32[8]{0:T(128)S(1)}, s32[8]{0:T(128)}, u32[]{:S(2)}) copy-start(s32[8]{0:T(128)} %param.28) | copy-start | bytes 100
  36.4 8.4 %copy-start.4 = (f32[1024]{0:T(1024)S(1)}, f32[1024]{0:T(1024)}, u32[]{:S(2)}) copy-start(f32[1024]{0:T(1024)} %param.24) | copy-start | bytes 12292
  36.4 8.4 %copy-start.5 = (f32[1024]{0:T(1024)S(1)}, f32[1024]{0:T(1024)}, u32[]{:S(2)}) copy-start(f32[1024]{0:T(1024)} %param.26) | copy-start | bytes 12292
  36.4 8.4 %copy-start.2 = (f32[3,1024]{1,0:T(4,128)S(1)}, f32[3,1024]{1,0:T(4,128)}, u32[]{:S(2)}) copy-start(f32[3,1024]{1,0:T(4,128)} %param.22) | copy-start | bytes 36868
  36.4 9.0 %copy-start.8 = (f32[4]{0:T(128)S(1)}, f32[4]{0:T(128)}, u32[]{:S(2)}) copy-start(f32[4]{0:T(128)} %constant.143.clone) | copy-start | bytes 52
  36.4 13.0 %copy-start.10 = (s32[128,2]{0,1:T(2,128)S(1)}, s32[128,2]{0,1:T(2,128)}, u32[]{:S(2)}) copy-start(s32[128,2]{0,1:T(2,128)} %param.33) | copy-start | bytes 3076
  36.5 7.6 %all-to-all-start.2 = ((f32[24,2,128]{2,1,0:T(2,128)}), f32[24,2,128]{2,1,0:T(2,128)S(1)}, u32[]{:S(2)}, u32[]{:S(2)}) async-start(f32[24,2,128]{2,1,0:T(2,128)} %bitcast.98), calls=%async_computation.2 | async-start | bytes 49152 | tf_op jit(solution)/shard_map/all_to_all | solution.py:146
  46.2 7.6 %all-to-all-start.3 = ((f32[24,4,128]{2,1,0:T(4,128)}), f32[24,4,128]{2,1,0:T(4,128)S(1)}, u32[]{:S(2)}, u32[]{:S(2)}) async-start(f32[24,4,128]{2,1,0:T(4,128)} %broadcast_select_fusion.2), calls=%async_computation.3 | async-start | bytes 98304 | tf_op jit(solution)/shard_map/all_to_all | solution.py:143
  59.1 7.5 %all-to-all-start.4 = ((f32[24,2,128]{2,1,0:T(2,128)}), f32[24,2,128]{2,1,0:T(2,128)S(1)}, u32[]{:S(2)}, u32[]{:S(2)}) async-start(f32[24,2,128]{2,1,0:T(2,128)} %bitcast.108), calls=%async_computation.4 | async-start | bytes 49152 | tf_op jit(solution)/shard_map/all_to_all | solution.py:146
  68.6 7.9 %all-to-all-start.5 = ((f32[24,4,128]{2,1,0:T(4,128)}), f32[24,4,128]{2,1,0:T(4,128)S(1)}, u32[]{:S(2)}, u32[]{:S(2)}) async-start(f32[24,4,128]{2,1,0:T(4,128)} %broadcast_select_fusion.1), calls=%async_computation.5 | async-start | bytes 98304 | tf_op jit(solution)/shard_map/all_to_all | solution.py:143
  77.1 39.9 %copy-start.7 = (f32[1024]{0:T(1024)S(1)}, f32[1024]{0:T(1024)}, u32[]{:S(2)}) copy-start(f32[1024]{0:T(1024)} %param.25) | copy-start | bytes 12292
  77.1 40.0 %copy-start.3 = (f32[3,1024]{1,0:T(4,128)S(1)}, f32[3,1024]{1,0:T(4,128)}, u32[]{:S(2)}) copy-start(f32[3,1024]{1,0:T(4,128)} %param.23) | copy-start | bytes 36868
  81.8 7.5 %all-to-all-start.6 = ((f32[24,2,128]{2,1,0:T(2,128)}), f32[24,2,128]{2,1,0:T(2,128)S(1)}, u32[]{:S(2)}, u32[]{:S(2)}) async-start(f32[24,2,128]{2,1,0:T(2,128)} %bitcast.116), calls=%async_computation.6 | async-start | bytes 49152 | tf_op jit(solution)/shard_map/all_to_all | solution.py:146
  89.3 43.1 %all-to-all-start.7 = ((s32[128,3,2]{1,2,0:T(2,128)}), s32[128,3,2]{1,2,0:T(2,128)S(1)}, u32[]{:S(2)}, u32[]{:S(2)}) async-start(s32[128,3,2]{1,2,0:T(2,128)} %copy.162), calls=%async_computation.7 | async-start | bytes 262144 | tf_op jit(solution)/shard_map/all_to_all | solution.py:167
  117.1 540.5 %copy-start.6 = (f32[8,1,128]{2,0,1:T(8,128)}, f32[8,1,128]{2,0,1:T(8,128)S(1)}, u32[]{:S(2)}) copy-start(f32[8,1,128]{2,0,1:T(8,128)S(1)} %get-tuple-element.305) | copy-start | bytes 12292
  117.2 1.9 copy-start.11
  132.4 147.8 %all-to-all-start.8 = ((f32[384,10,128]{2,1,0:T(8,128)}), f32[384,10,128]{2,1,0:T(8,128)S(1)}, u32[]{:S(2)}, u32[]{:S(2)}) async-start(f32[384,10,128]{2,1,0:T(8,128)} %broadcast_select_fusion), calls=%async_computation.8 | async-start | bytes 6291456 | tf_op jit(solution)/shard_map/all_to_all | solution.py:179
  639.9 14.0 %copy-start.9 = (s32[128,1]{0,1:T(1,128)S(1)}, s32[128,1]{0,1:T(1,128)}, u32[]{:S(2)}) copy-start(s32[128,1]{0,1:T(1,128)} %param.32) | copy-start | bytes 1540
  642.5 52.8 %all-to-all-start.9 = ((f32[384,4,128]{2,1,0:T(4,128)}), f32[384,4,128]{2,1,0:T(4,128)S(1)}, u32[]{:S(2)}, u32[]{:S(2)}) async-start(f32[384,4,128]{2,1,0:T(4,128)} %copy.172), calls=%async_computation.9 | async-start | bytes 1572864 | tf_op jit(solution)/shard_map/all_to_all | solution.py:182
where the time goes:
time: 703 us; the launch traced here: 698 us
  other arithmetic  346 us (49%)
  waiting for transfers between devices  184 us (26%)
  local copies, waits for them, and re-layouts  92.4 us (13%)
  starting transfers between devices  71.3 us (10%)
    reduce_sum x25, other arithmetic, force_tile(): jnp.sum(push * deltas[0], -1)  156 us
    reduce_sum x25, other arithmetic, force_tile(): jnp.sum(heat, -1)  148 us
    all_to_all x1, waiting for transfers between devices, on_device(): lax.all_to_all(sent_state, 'wide', split_axis=0, concat_axis=0, tiled=True)  122 us
    squeeze x54, local copies, waits for them, and re-layouts, grouped(): lax.map(lambda pair: kernel(pair[0], pair[1]), (shaped_t, shaped_s))  44.1 us
    all_to_all x1, waiting for transfers between devices, on_device(): lax.all_to_all(partial_value, 'wide', split_axis=0, concat_axis=0, tiled=...  34.4 us
    all_to_all x1, starting transfers between devices, on_device(): lax.all_to_all(force_near[force_entry], 'wide', split_axis=0, concat_axis...  27 us
    dynamic_update_slice x24, other arithmetic, grouped(): lax.map(lambda pair: kernel(pair[0], pair[1]), (shaped_t, shaped_s))  15 us
  transfers between devices with their start and end apart: 10, of which 9 were waited for; matrix products, arithmetic and copies ran while one was open for 7% of the time, Pallas kernels for 0%

commit v1 on v0

v1 whole, which is shorter than its diff:
```python
import functools
import math

import jax
import jax.numpy as jnp
from jax import lax
from jax.experimental import pallas as pl
from jax.experimental.pallas import tpu as pltpu
from jax.sharding import PartitionSpec as P

F32, BF16 = jnp.float32, jnp.bfloat16
MESH = pl.DeviceIdType.MESH

PASSES = 3
KERNEL_NORM = math.pi ** (-1.5)
TARGET_COUNT = 24.0
LOG2E = math.log2(math.e)

NB = 8
BLK = 128
NZ, NX, NC, NY = 16, 4, 2, 4
XN = 8
XW = 128
ITEMS = NB + XW
KF = 64

Z_ORDER = [0]
for _d in range(1, NZ // 2):
    Z_ORDER += [_d, -_d]
Z_ORDER.append(NZ // 2)
Z_PLACE = {d % NZ: p for p, d in enumerate(Z_ORDER)}
BATCHES = ((0, 1), (1, 5), (5, 9), (9, 13), (13, 16))


def remote(src, dst, send, recv, device):
    return pltpu.make_async_remote_copy(
        src_ref=src,
        dst_ref=dst,
        send_sem=send,
        recv_sem=recv,
        device_id=device,
        device_id_type=MESH,
    )


class Gather:
    def __init__(self, own, out, zs, zr, xs, xr, cs, cr, lsem):
        self.own, self.out = own, out
        self.zs, self.zr, self.xs, self.xr, self.cs, self.cr = zs, zr, xs, xr, cs, cr
        self.lsem = lsem
        w = lax.axis_index("wide")
        self.z, self.x, self.c = w // (NX * NC), (w // NC) % NX, w % NC
        self.sent = []

    def device(self, dz, dx, dc):
        z = (self.z + dz) % NZ
        x = (self.x + dx) % NX
        c = (self.c + dc) % NC
        return {"wide": (z * NX + x) * NC + c}

    def go(self, copy):
        copy.start()
        self.sent.append(copy)

    def start(self):
        self.local = pltpu.make_async_copy(self.own, self.out.at[0, 0, 0], self.lsem)
        self.local.start()
        for d in Z_ORDER[1:]:
            place = Z_PLACE[-d % NZ]
            self.go(
                remote(
                    self.own,
                    self.out.at[0, 0, place],
                    self.zs.at[place],
                    self.zr.at[place],
                    self.device(d, 0, 0),
                )
            )
        self.local.wait()
        self.forward_x(0)
        self.forward_core(0, 0)

    def wait_z(self, batch):
        for place in range(*BATCHES[batch]):
            if place > 0:
                remote(
                    self.own,
                    self.out.at[0, 0, place],
                    self.zs.at[place],
                    self.zr.at[place],
                    self.device(1, 0, 0),
                ).wait_recv()

    def part(self, core, x, batch):
        lo, hi = BATCHES[batch]
        return self.out.at[core, x, pl.ds(lo, hi - lo)]

    def x_copy(self, batch, k):
        j = NX - k
        return remote(
            self.part(0, 0, batch),
            self.part(0, j, batch),
            self.xs.at[j, batch],
            self.xr.at[j, batch],
            self.device(0, k, 0),
        )

    def forward_x(self, batch):
        for k in (2, 1, 3):
            self.go(self.x_copy(batch, k))

    def core_copy(self, x, batch):
        return remote(
            self.part(0, x, batch),
            self.part(1, x, batch),
            self.cs.at[x, batch],
            self.cr.at[x, batch],
            self.device(0, 0, 1),
        )

    def forward_core(self, x, batch):
        self.go(self.core_copy(x, batch))

    def z_step(self, batch):
        self.wait_z(batch)
        self.forward_x(batch)
        self.forward_core(0, batch)

    def x_step(self, batch):
        for k in (1, 3, 2):
            self.x_copy(batch, k).wait_recv()
            self.forward_core(NX - k, batch)

    def finish(self):
        for batch in range(len(BATCHES)):
            for x in range(NX):
                self.core_copy(x, batch).wait_recv()
        for copy in self.sent:
            copy.wait_send()


def first_sums(item, target, sources, slope, r2_ref, mx_ref, tot_ref, mom_ref):
    tot = mom = 0.0
    for s, source in enumerate(sources):
        cols = source.T
        r2 = 0.0
        for q in range(3):
            delta = target[q : q + 1] - cols[:, q : q + 1]
            r2 = r2 + delta * delta
        mass = jnp.broadcast_to(cols[:, 6:7], (BLK, BLK))
        r2_ref[item, pl.ds(s * BLK, BLK)] = r2
        mx_ref[item, pl.ds(s * BLK, BLK)] = mass
        weight = jnp.exp2(r2 * slope) * mass
        tot = tot + jnp.sum(weight, axis=0, keepdims=True)
        mom = mom + jnp.sum(weight * r2, axis=0, keepdims=True)
    tot_ref[pl.ds(item, 1)] = tot
    mom_ref[pl.ds(item, 1)] = mom


def next_sums(item, slope, r2_ref, mx_ref, tot_ref, mom_ref):
    r2 = r2_ref[item]
    weight = jnp.exp2(r2 * slope) * mx_ref[item]
    tot_ref[pl.ds(item, 1)] = jnp.sum(weight, axis=0, keepdims=True)
    mom_ref[pl.ds(item, 1)] = jnp.sum(weight * r2, axis=0, keepdims=True)


def gather_kernel(
    near,
    dens_block,
    dens_source,
    own,
    mass,
    width_in,
    dens_rows,
    e_out,
    l_out,
    beside,
    r2_ref,
    mx_ref,
    tot_ref,
    mom_ref,
    slope_ref,
    late,
    ys,
    yr,
    *sems,
):
    half = len(sems) // 2
    early_gather = Gather(own, e_out, *sems[:half])
    late_gather = Gather(late, l_out, *sems[half:])
    n = lax.axis_index("narrow")

    barrier = pltpu.get_barrier_semaphore()
    partners = [{"narrow": (n + k) % NY} for k in range(1, NY)]
    partners += [early_gather.device(0, 0, 1)]
    partners += [early_gather.device(0, k, 0) for k in range(1, NX)]
    partners += [early_gather.device(d, 0, 0) for d in Z_ORDER[1:]]
    for device in partners:
        pl.semaphore_signal(barrier, inc=1, device_id=device, device_id_type=MESH)

    def set_slope(width):
        slope = -LOG2E / (width * width)
        for b in range(NB):
            slope_ref[b] = slope[b : b + 1]

    width = width_in[...]
    set_slope(width)

    def local_first(item, carry):
        target = own[item]
        first_sums(
            item,
            target,
            (target, own[near[item]]),
            slope_ref[item],
            r2_ref,
            mx_ref,
            tot_ref,
            mom_ref,
        )
        return carry

    lax.fori_loop(0, NB, local_first, 0)
    beside[pl.ds(0, NB)] = own[...]

    pl.semaphore_wait(barrier, len(partners))

    y_copies = []
    for k in range(1, NY):
        y_copies.append(
            remote(
                own,
                beside.at[pl.ds((NY - k) * NB, NB)],
                ys.at[NY - k],
                yr.at[NY - k],
                {"narrow": (n + k) % NY},
            )
        )
        y_copies[-1].start()
    early_gather.start()
    for copy in y_copies:
        copy.wait_recv()

    def export_first(e, carry):
        block = dens_block[e]
        first_sums(
            NB + e,
            own[block],
            (beside[dens_source[2 * e]], beside[dens_source[2 * e + 1]]),
            slope_ref[block],
            r2_ref,
            mx_ref,
            tot_ref,
            mom_ref,
        )
        return carry

    lax.fori_loop(0, XN, export_first, 0)

    def combined(ref):
        value = ref[pl.ds(0, NB)]
        for e in range(XN):
            value = value + dens_rows[e] * ref[pl.ds(NB + e, 1)]
        return value

    for step in range(PASSES):
        if step > 0:

            def local_next(item, carry):
                next_sums(item, slope_ref[item], r2_ref, mx_ref, tot_ref, mom_ref)
                return carry

            def export_next(e, carry):
                next_sums(NB + e, slope_ref[dens_block[e]], r2_ref, mx_ref, tot_ref, mom_ref)
                return carry

            lax.fori_loop(0, NB, local_next, 0)
            lax.fori_loop(0, XN, export_next, 0)
        total = combined(tot_ref)
        if step + 1 < PASSES:
            moment = combined(mom_ref)
            ratio = jnp.log(KERNEL_NORM * total / (TARGET_COUNT * mass[...]))
            bend = 2.0 * moment / (width * width * total)
            width = width * jnp.exp(-ratio / (3.0 + bend))
            set_slope(width)

    late[pl.ds(0, NB)] = width
    late[pl.ds(NB, NB)] = KERNEL_NORM * total / (width * width * width)
    late_gather.start()

    early_gather.z_step(1)
    early_gather.x_step(0)
    early_gather.z_step(2)
    early_gather.x_step(1)
    early_gather.z_step(3)
    late_gather.x_step(0)
    early_gather.x_step(2)
    early_gather.z_step(4)
    late_gather.z_step(1)
    early_gather.x_step(3)
    late_gather.z_step(2)
    late_gather.z_step(3)
    late_gather.z_step(4)
    early_gather.x_step(4)
    for batch in range(1, 5):
        late_gather.x_step(batch)
    early_gather.finish()
    late_gather.finish()
    for copy in y_copies:
        copy.wait_send()


def gather_call(near, dens_block, dens_source, own, mass, width, dens_rows):
    smem = pl.BlockSpec(memory_space=pltpu.SMEM)
    vmem = pl.BlockSpec(memory_space=pltpu.VMEM)
    batches = len(BATCHES)
    dma = pltpu.SemaphoreType.DMA
    per_gather = [dma((NZ,)), dma((NZ,))] + [dma((NX, batches))] * 4 + [dma]
    return pl.pallas_call(
        gather_kernel,
        out_shape=(
            jax.ShapeDtypeStruct((NC, NX, NZ, NB, 8, BLK), F32),
            jax.ShapeDtypeStruct((NC, NX, NZ, 2 * NB, BLK), F32),
        ),
        in_specs=[smem] * 3 + [vmem] * 4,
        out_specs=(pl.BlockSpec(memory_space=pl.ANY),) * 2,
        scratch_shapes=[
            pltpu.VMEM((NY * NB, 8, BLK), F32),
            pltpu.VMEM((NB + XN, 2 * BLK, BLK), F32),
            pltpu.VMEM((NB + XN, 2 * BLK, BLK), F32),
            pltpu.VMEM((NB + XN, BLK), F32),
            pltpu.VMEM((NB + XN, BLK), F32),
            pltpu.VMEM((NB, 1, BLK), F32),
            pltpu.VMEM((2 * NB, BLK), F32),
            dma((NY,)),
            dma((NY,)),
        ]
        + per_gather * 2,
        compiler_params=pltpu.CompilerParams(
            collective_id=0, has_side_effects=True, vmem_limit_bytes=32 * 2**20
        ),
        name="density_and_gather",
    )(near, dens_block, dens_source, own, mass, width, dens_rows)


def split_two(value):
    high = value.astype(BF16).astype(F32)
    return high, value - high


def split_three(value):
    high, rest = split_two(value)
    return (high,) + split_two(rest)


def target_features(tile):
    row = lax.broadcasted_iota(jnp.int32, tile.shape, 0)
    swapped = jnp.where(row < 3, pltpu.roll(tile, 5, 0), pltpu.roll(tile, 3, 0))
    squares = jnp.sum(jnp.where(row < 3, tile * tile, 0.0), axis=0, keepdims=True)
    crosses = jnp.sum(jnp.where(row < 3, tile * swapped, 0.0), axis=0, keepdims=True)
    distance = jnp.where(row < 3, -2.0 * tile, jnp.where(row == 6, 1.0, 0.0))
    approach = jnp.where(row < 6, -40.0 * swapped, jnp.where(row == 7, 40.0, 0.0))
    outs = []
    for factor, constant in ((distance, squares), (approach, 40.0 * crosses)):
        h, m, l = split_three(factor)
        ch, cm, cl = split_three(constant)
        constants = jnp.where(row == 0, ch, jnp.where(row == 1, cm, jnp.where(row == 2, cl, 0.0)))
        full = jnp.concatenate([h, m, l, h, m, h, constants] + [jnp.zeros_like(h)] * 9, axis=0)
        outs.append(full.T)
    return jnp.concatenate(outs, axis=0).astype(BF16)[:, :KF]


T_SQ, T_CROSS, T_EXP, T_SCALE, T_WIDTH, T_SOUND, T_RHO, T_PRESS = range(8)


def slot_table(tab_ref, slot, tiles_ref, late_ref):
    def column(q):
        return tiles_ref[slot, pl.ds(q, NB, stride=8)]

    x, y, z, vx, vy, vz = (column(q) for q in range(6))
    energy = column(7)
    width = late_ref[slot, pl.ds(0, NB)]
    rho = late_ref[slot, pl.ds(NB, NB)]
    tab_ref[slot, T_SQ] = x * x + y * y + z * z
    tab_ref[slot, T_CROSS] = x * vx + y * vy + z * vz
    tab_ref[slot, T_EXP] = -LOG2E / (width * width)
    tab_ref[slot, T_SCALE] = math.log2(2.0 * KERNEL_NORM) - 5.0 * jnp.log2(width)
    tab_ref[slot, T_WIDTH] = 0.05 * width
    tab_ref[slot, T_SOUND] = jnp.sqrt((10.0 / 9.0) * energy)
    tab_ref[slot, T_RHO] = 8.0 * rho
    tab_ref[slot, T_PRESS] = (2.0 / 3.0) * energy / rho


TARGET_VALUES = (T_EXP, T_SCALE, T_WIDTH, T_SOUND, T_RHO, T_PRESS)


def force_kernel(
    blk,
    sa,
    sb,
    tiles_ref,
    late_ref,
    rho_out,
    acc_out,
    heat_out,
    tab_ref,
    tl_ref,
    tg_ref,
    acc_ref,
    r0,
    r1,
    f0,
    f1,
    w0,
    w1,
):
    slots = tiles_ref.shape[0]

    def fill(slot, carry):
        slot_table(tab_ref, slot, tiles_ref, late_ref)
        return carry

    lax.fori_loop(0, slots, fill, 0)

    def prepare(b, carry):
        tl_ref[b] = target_features(tiles_ref[0, pl.ds(pl.multiple_of(b * 8, 8), 8)])
        for i, q in enumerate(TARGET_VALUES):
            tg_ref[b, i] = jnp.broadcast_to(tab_ref[0, q, pl.ds(b, 1)], (BLK, BLK)).T
        acc_ref[b] = jnp.zeros((16, 2 * BLK), F32)
        return carry

    lax.fori_loop(0, NB, prepare, 0)
    f1[...] = jnp.zeros(f1.shape, BF16)
    w1[...] = jnp.zeros(w1.shape, BF16)

    def pick(i, q):
        a, b = sa[i], sb[i]
        return jnp.concatenate(
            [tab_ref[a // NB, q, pl.ds(a % NB, 1)], tab_ref[b // NB, q, pl.ds(b % NB, 1)]], axis=1
        )

    def products(i, r_ref, f_ref):
        a, b = sa[i], sb[i]
        raw = jnp.concatenate(
            [
                tiles_ref[s // NB, pl.ds(pl.multiple_of((s % NB) * 8, 8), 8)]
                for s in (a, b)
            ],
            axis=1,
        )
        row = lax.broadcasted_iota(jnp.int32, raw.shape, 0)
        cross = pick(i, T_CROSS)
        u = jnp.where(row < 6, raw, jnp.where(row == 6, pick(i, T_SQ), cross))
        h, m, l = split_three(u)
        feats = jnp.concatenate([h, h, h, m, m, l, jnp.ones_like(h), jnp.zeros_like(h)], axis=0)
        r_ref[...] = jnp.dot(tl_ref[blk[i]], feats.astype(BF16), preferred_element_type=F32)
        f = jnp.where(row == 6, 1.0, u) * raw[6:7]
        f_ref[...] = jnp.concatenate(split_two(f), axis=0).astype(BF16)

    def pairs(i, r_ref, w_ref):
        b = blk[i]
        exp_j, scale_j, width_j, sound_j, rho_j, press_j = (pick(i, q) for q in TARGET_VALUES)
        for g in range(8):
            r2 = r_ref[pl.ds(16 * g, 16)]
            vd = r_ref[pl.ds(BLK + 16 * g, 16)]

            def own(q):
                value = tg_ref[b, q, pl.ds(16 * g, 16)]
                return jnp.concatenate([value, value], axis=1)

            hs = own(2) + width_j
            nu = jnp.minimum(hs * vd * pl.reciprocal(r2 + hs * hs, approx=True), 0.0)
            visc = nu * (nu - (own(3) + sound_j)) * pl.reciprocal(own(4) + rho_j, approx=True)
            grad_i = jnp.exp2(r2 * own(0) + own(1))
            grad_j = jnp.exp2(r2 * exp_j + scale_j)
            first = own(5) * grad_i
            both = first + visc * (grad_i + grad_j)
            w_ref[pl.ds(16 * g, 16)] = (both + press_j * grad_j).astype(BF16)
            w_ref[pl.ds(BLK + 16 * g, 16)] = (both + first).astype(BF16)

    def reduce(i, f_ref, w_ref):
        b = blk[i]
        acc_ref[b] = acc_ref[b] + lax.dot_general(
            f_ref[...], w_ref[...], (((1,), (1,)), ((), ())), preferred_element_type=F32
        )

    products(0, r0, f0)

    def body(k, carry):
        i = 2 * k
        reduce(jnp.maximum(i - 1, 0), f1, w1)
        products(i + 1, r1, f1)
        pairs(i, r0, w0)
        reduce(i, f0, w0)
        products(jnp.minimum(i + 2, ITEMS - 1), r0, f0)
        pairs(i + 1, r1, w1)
        return carry

    lax.fori_loop(0, ITEMS // 2, body, 0)
    reduce(ITEMS - 1, f1, w1)

    rho_out[...] = late_ref[0, pl.ds(NB, NB)]
    for b in range(NB):
        tile = tiles_ref[0, pl.ds(8 * b, 8)]
        s = acc_ref[b]
        s = s[0:8] + s[8:16]
        push, heat = s[:, 0:BLK], s[:, BLK:]
        for q in range(3):
            acc_out[q, pl.ds(b, 1)] = tile[q : q + 1] * push[6:7] - push[q : q + 1]
        value = tab_ref[0, T_CROSS, pl.ds(b, 1)] * heat[6:7] + heat[7:8]
        for q in range(3):
            value = value - tile[3 + q : 4 + q] * heat[q : q + 1]
            value = value - tile[q : q + 1] * heat[3 + q : 4 + q]
        heat_out[pl.ds(b, 1)] = -0.5 * value


def force_call(blk, sa, sb, tiles, late):
    smem = pl.BlockSpec(memory_space=pltpu.SMEM)
    vmem = pl.BlockSpec(memory_space=pltpu.VMEM)
    slots = NC * NX * NZ
    return pl.pallas_call(
        force_kernel,
        out_shape=(
            jax.ShapeDtypeStruct((NB, BLK), F32),
            jax.ShapeDtypeStruct((3, NB, BLK), F32),
            jax.ShapeDtypeStruct((NB, BLK), F32),
        ),
        in_specs=[smem] * 3 + [vmem] * 2,
        out_specs=(vmem,) * 3,
        scratch_shapes=[
            pltpu.VMEM((slots, 8, NB, BLK), F32),
            pltpu.VMEM((NB, 2 * BLK, KF), BF16),
            pltpu.VMEM((NB, 6, BLK, BLK), F32),
            pltpu.VMEM((NB, 16, 2 * BLK), F32),
            pltpu.VMEM((2 * BLK, 2 * BLK), F32),
            pltpu.VMEM((2 * BLK, 2 * BLK), F32),
            pltpu.VMEM((16, 2 * BLK), BF16),
            pltpu.VMEM((16, 2 * BLK), BF16),
            pltpu.VMEM((2 * BLK, 2 * BLK), BF16),
            pltpu.VMEM((2 * BLK, 2 * BLK), BF16),
        ],
        compiler_params=pltpu.CompilerParams(vmem_limit_bytes=40 * 2**20),
        name="force",
    )(blk, sa, sb, tiles, late)


def on_device(
    position,
    velocity,
    mass,
    energy,
    smoothing,
    local_near,
    dens_block,
    dens_dest,
    dens_near,
    force_block,
    force_dest,
    force_near,
):
    fields = jnp.concatenate([position, velocity, mass[None], energy[None]], axis=0)
    own = fields.reshape(8, NB, BLK).transpose(1, 0, 2)
    blocks = jnp.arange(NB, dtype=jnp.int32)
    row = (dens_dest - lax.axis_index("narrow") + NY) % NY
    dens_rows = jnp.broadcast_to(
        (dens_block[:, None] == blocks[None, :]).astype(F32)[:, :, None], (XN, NB, BLK)
    )
    tiles, late = gather_call(
        local_near,
        dens_block,
        (row * NB + dens_near).reshape(-1),
        own,
        mass.reshape(NB, BLK),
        smoothing.reshape(NB, BLK),
        dens_rows,
    )
    w = lax.axis_index("wide")
    z, x, c = w // (NX * NC), (w // NC) % NX, w % NC
    there = force_dest[:, 0]
    dz = (there // (NX * NC) - z + NZ) % NZ
    place = jnp.where(dz == 0, 0, jnp.where(dz <= NZ // 2, 2 * dz - 1, 2 * (NZ - dz)))
    dx = ((there // NC) % NX - x + NX) % NX
    dc = (there % NC - c + NC) % NC
    slot = (dc * NX + dx) * NZ + place
    blk = jnp.concatenate([blocks, force_block])
    sa = jnp.concatenate([blocks, slot * NB + force_near[:, 0]])
    sb = jnp.concatenate([local_near, slot * NB + force_near[:, 1]])
    slots = NC * NX * NZ
    rho, accel, heat = force_call(
        blk, sa, sb, tiles.reshape(slots, 8 * NB, BLK), late.reshape(slots, 2 * NB, BLK)
    )
    return rho.reshape(NB * BLK), accel.reshape(3, NB * BLK), heat.reshape(NB * BLK)


def solution(mesh):
    both = ("wide", "narrow")
    in_specs = (
        P(None, both),
        P(None, both),
        P(both),
        P(both),
        P(both),
        P(both),
        P(both),
        P(both, None),
        P(both, None),
        P(both),
        P(both, None),
        P(both, None),
    )
    out_specs = (P(both), P(None, both), P(both))
    return jax.shard_map(
        on_device, mesh=mesh, in_specs=in_specs, out_specs=out_specs, check_vma=False
    )
```

time: 703 us -> 96.1 us (0.14)
  other arithmetic: 346 us -> 5.01 us
  waiting for transfers between devices: 184 us -> 0 us
  local copies, waits for them, and re-layouts: 92.4 us -> 3.53 us
  Pallas kernels: 0 us -> 86.6 us
  starting transfers between devices: 71.3 us -> 0 us
    reduce_sum x63 -> x0, other arithmetic: 318 us -> none  [the longest x25 156 us: force_tile(): jnp.sum(push * deltas[0], -1)]
    all_to_all x10 -> x0, waiting for transfers between devices: 184 us -> none  [the longest x1 122 us: on_device(): lax.all_to_all(sent_state, 'wide', split_axis=0, concat_axis=0, tiled=True)]
    pallas_call x0 -> x2, Pallas kernels: none -> 86.6 us  [the longest x1 58.8 us: gather_call(): pl.pallas_call(gather_kernel, out_shape=(jax.ShapeDtypeStruct((NC, NX, NZ...]
    all_to_all x10 -> x0, starting transfers between devices: 71.3 us -> none  [the longest x1 27 us: on_device(): lax.all_to_all(force_near[force_entry], 'wide', split_axis=0, concat_axis...]
    squeeze x54 -> x0, local copies, waits for them, and re-layouts: 44.1 us -> none  [grouped(): lax.map(lambda pair: kernel(pair[0], pair[1]), (shaped_t, shaped_s))]
    gather x20 -> x0, local copies, waits for them, and re-layouts: 24.1 us -> none  [the longest x2 10.2 us: on_device(): force_served = join_blocks(force_source[force_wanted])]
    dynamic_update_slice x24 -> x0, other arithmetic: 15 us -> none  [grouped(): lax.map(lambda pair: kernel(pair[0], pair[1]), (shaped_t, shaped_s))]
    another operation x6 -> x0, local copies, waits for them, and re-layouts: 9 us -> none  [the longest x2 6.59 us: grouped(): shaped_s = source.reshape((items // group, group) + source.shape[1:])]
  transfers between devices with their start and end apart: 10 -> 0, of which waited for: 9 -> 0; matrix products, arithmetic and copies ran while one was open for 7% -> 0% of each run, Pallas kernels for 0% -> 0%
where the time goes in v1:
time: 96.1 us; the launch traced here: 95.8 us
  Pallas kernels  86.6 us (90%)
  other arithmetic  5.01 us (5%)
  local copies, waits for them, and re-layouts  3.53 us (4%)
    pallas_call x1, Pallas kernels, gather_call(): pl.pallas_call(gather_kernel, out_shape=(jax.ShapeDtypeStruct((NC, NX, NZ...  58.8 us
    pallas_call x1, Pallas kernels, force_call(): pl.pallas_call(force_kernel, out_shape=(jax.ShapeDtypeStruct((NB, BLK), F...  27.8 us
    unnamed x9, local copies, waits for them, and re-layouts  3.29 us

profile of v1, /device:TPU:1, one launch (start us, length us, event | category | flops | bytes accessed | tf_op | source)
XLA Modules:
  0.0 95.8 jit_solution(779996876847951721)
XLA Ops:
  0.7 0.7 bitcast_add_fusion
  1.4 0.7 fusion.9
  2.1 0.7 broadcast_add_fusion
  2.7 0.7 bitcast_add_fusion.1
  3.4 0.7 pad_add_fusion
  4.2 0.1 copy.16
  4.2 0.1 reshape.59.dens_source
  4.3 0.7 fusion
  5.1 0.1 broadcast_in_dim.3.dens_rows
  5.1 0.8 maximum_bitcast_fusion.own
  5.9 0.0 copy-start
  5.9 0.7 copy-done
  6.6 0.0 copy-start.1
  6.6 0.7 copy-done.1
  7.3 0.0 copy-start.2
  7.3 0.7 copy-done.2
  8.0 0.0 copy-start.3
  8.0 0.7 copy-done.3
  8.6 58.8 %density_and_gather.1 = (f32[2,4,16,8,8,128]{5,4,3,2,1,0:T(8,128)S(1)}, f32[2,4,16,16,128]{4,3,2,1,0:T(8,128)S(1)}) custom-call(s32[8]{0:T(128)S(1)} %copy-done.3, s32[8]{0:T(128)S(1)} %copy-done.2, s32[16]{0:T(128)S(1)} %reshape.59.dens_source, f32[8,8,128]{2,1,0:T(8,128)S(1)} %maximum_bitcast_fusion.own, f32[8,128]{1,0:T(8,128)S(1)} %bitcast.44, ...), custom_call_target="tpu_custom_call" | custom-call | tf_op jit(solution)/shard_map/density_and_gather/pallas_call | solution.py:319
  67.4 27.8 %force.1 = (f32[8,128]{1,0:T(8,128)}, f32[3,8,128]{2,1,0:T(8,128)S(1)}, f32[8,128]{1,0:T(8,128)}) custom-call(s32[136]{0:T(256)S(1)} %get-tuple-element.16.blk, s32[136]{0:T(256)S(1)} %get-tuple-element.15.sa, s32[136]{0:T(256)S(1)} %get-tuple-element.17.sb, f32[128,64,128]{2,1,0:T(8,128)S(1)} %bitcast.41, f32[128,16,128]{2,1,0:T(8,128)S(1)} %bitcast.42), custom_call_target="tpu_custom_call" | custom-call | tf_op jit(solution)/shard_map/force/pallas_call | solution.py:521
  95.2 0.6 copy.19
  (1 shorter events, 0.0 us)
Async XLA Ops:
  5.9 0.7 copy-start
  6.6 0.7 copy-start.1
  7.3 0.7 copy-start.2
  8.0 0.7 copy-start.3

commit v2 on v1

v2 whole, which is shorter than its diff:
```python
import functools
import math

import jax
import jax.numpy as jnp
from jax import lax
from jax.experimental import pallas as pl
from jax.experimental.pallas import tpu as pltpu
from jax.sharding import PartitionSpec as P

F32, BF16 = jnp.float32, jnp.bfloat16
MESH = pl.DeviceIdType.MESH

PASSES = 3
KERNEL_NORM = math.pi ** (-1.5)
TARGET_COUNT = 24.0
LOG2E = math.log2(math.e)

NB = 8
BLK = 128
NZ, NX, NC, NY = 16, 4, 2, 4
XN = 8
XW = 128
ITEMS = NB + XW
CHUNKS = 8
KF = 64

RELAY = 4
Z_ORDER = [0, 4, -4, 1, -1, 2, -2, 3, -3, 5, -5, 6, -6, 7, -7, 8]
Z_PLACE = {d % NZ: p for p, d in enumerate(Z_ORDER)}
BATCHES = ((0, 1), (1, 5), (5, 9), (9, 13), (13, 16))
FAR = Z_PLACE[NZ // 2]


def remote(src, dst, send, recv, device):
    return pltpu.make_async_remote_copy(
        src_ref=src,
        dst_ref=dst,
        send_sem=send,
        recv_sem=recv,
        device_id=device,
        device_id_type=MESH,
    )


AFTER_FIRST_PASS = ("Ez1",)
BEFORE_LAST_PASS = ("En0",)
AFTER_DENSITY = (
    "Ez2", "En1", "Ef0", "Ez3", "Ez4", "En2", "Ef1", "En3",
    "Lz1", "Lz2", "Ef2", "En4", "Ln0", "Lf0", "Lz3", "Lz4",
    "Ef3", "Ln1", "Lf1", "Ef4", "Ln2", "Lf2", "Ln3", "Lf3",
    "Ln4", "Lf4",
)


class Gather:
    def __init__(self, own, out, halved, zs, zr, xs, xr, cs, cr, lsem):
        self.own, self.out, self.halved = own, out, halved
        self.zs, self.zr, self.xs, self.xr, self.cs, self.cr = zs, zr, xs, xr, cs, cr
        self.lsem = lsem
        w = lax.axis_index("wide")
        self.z, self.x, self.c = w // (NX * NC), (w // NC) % NX, w % NC
        self.half = own.shape[0] // 2
        self.sent = []

    def device(self, dz, dx, dc):
        z = (self.z + dz + NZ) % NZ
        x = (self.x + dx + NX) % NX
        c = (self.c + dc) % NC
        return {"wide": (z * NX + x) * NC + c}

    def go(self, copy):
        copy.start()
        self.sent.append(copy)

    def halves(self, ref, side):
        return ref.at[pl.ds(side * self.half, self.half)]

    def z_copy(self, src, distance, hop, side=None):
        place = Z_PLACE[distance % NZ]
        dst, sem = self.out.at[0, 0, place], place
        if side is not None:
            src, dst = self.halves(src, side), self.halves(dst, side)
            sem = place + side
        return remote(src, dst, self.zs.at[sem], self.zr.at[sem], self.device(hop, 0, 0))

    def start(self):
        self.local = pltpu.make_async_copy(self.own, self.out.at[0, 0, 0], self.lsem)
        self.local.start()
        for d in Z_ORDER[1:]:
            if abs(d) <= RELAY:
                self.go(self.z_copy(self.own, -d, d))
        self.local.wait()
        self.forward_x(0)
        self.forward_core(0, 0)

    def wait_z(self, batch):
        for place in range(*BATCHES[batch]):
            if place == FAR:
                for side in range(2):
                    self.z_copy(self.own, NZ // 2, 1, side).wait_recv()
            elif place > 0:
                self.z_copy(self.own, Z_ORDER[place], 1).wait_recv()

    def relay_z(self):
        for sign, side in ((1, 0), (-1, 1)):
            src = self.out.at[0, 0, Z_PLACE[-sign * RELAY % NZ]]
            for k in range(1, NZ // 2 - RELAY):
                self.go(self.z_copy(src, -sign * (RELAY + k), sign * k))
            self.go(self.z_copy(src, NZ // 2, sign * (NZ // 2 - RELAY), side))

    def part(self, core, x, batch, side=None):
        lo, hi = BATCHES[batch]
        if side is None:
            return self.out.at[core, x, pl.ds(lo, hi - lo)]
        return self.out.at[core, x, pl.ds(lo, hi - lo), pl.ds(side * self.half, self.half)]

    def x_copy(self, batch, k):
        j = NX - k
        return remote(
            self.part(0, 0, batch),
            self.part(0, j, batch),
            self.xs.at[j, batch],
            self.xr.at[j, batch],
            self.device(0, k, 0),
        )

    def x_relay(self, batch, side):
        sign = 1 - 2 * side
        sem = 2 * side
        return remote(
            self.part(0, (NX - sign) % NX, batch, side),
            self.part(0, 2, batch, side),
            self.xs.at[sem, batch],
            self.xr.at[sem, batch],
            self.device(0, sign, 0),
        )

    def forward_x(self, batch):
        for k in (1, 3) if self.halved else (2, 1, 3):
            self.go(self.x_copy(batch, k))

    def core_copy(self, x, batch):
        return remote(
            self.part(0, x, batch),
            self.part(1, x, batch),
            self.cs.at[x, batch],
            self.cr.at[x, batch],
            self.device(0, 0, 1),
        )

    def forward_core(self, x, batch):
        self.go(self.core_copy(x, batch))

    def z_step(self, batch):
        self.wait_z(batch)
        if batch == 1:
            self.relay_z()
        self.forward_x(batch)
        self.forward_core(0, batch)

    def x_near(self, batch):
        for k, side in ((1, 0), (3, 1)):
            self.x_copy(batch, k).wait_recv()
            if self.halved:
                self.go(self.x_relay(batch, side))
        self.forward_core(1, batch)
        self.forward_core(3, batch)

    def x_far(self, batch):
        if self.halved:
            for side in range(2):
                self.x_relay(batch, side).wait_recv()
        else:
            self.x_copy(batch, 2).wait_recv()
        self.forward_core(2, batch)

    def finish(self):
        for batch in range(len(BATCHES)):
            for x in range(NX):
                self.core_copy(x, batch).wait_recv()
        for copy in self.sent:
            copy.wait_send()


def first_sums(item, target, sources, slope, r2_ref, mx_ref, tot_ref, mom_ref):
    tot = mom = 0.0
    for s, source in enumerate(sources):
        cols = source.T
        r2 = 0.0
        for q in range(3):
            delta = target[q : q + 1] - cols[:, q : q + 1]
            r2 = r2 + delta * delta
        mass = jnp.broadcast_to(cols[:, 6:7], (BLK, BLK))
        r2_ref[item, pl.ds(s * BLK, BLK)] = r2
        mx_ref[item, pl.ds(s * BLK, BLK)] = mass
        weight = jnp.exp2(r2 * slope) * mass
        tot = tot + jnp.sum(weight, axis=0, keepdims=True)
        mom = mom + jnp.sum(weight * r2, axis=0, keepdims=True)
    tot_ref[pl.ds(item, 1)] = tot
    mom_ref[pl.ds(item, 1)] = mom


def next_sums(item, slope, r2_ref, mx_ref, tot_ref, mom_ref):
    r2 = r2_ref[item]
    weight = jnp.exp2(r2 * slope) * mx_ref[item]
    tot_ref[pl.ds(item, 1)] = jnp.sum(weight, axis=0, keepdims=True)
    mom_ref[pl.ds(item, 1)] = jnp.sum(weight * r2, axis=0, keepdims=True)


def gather_kernel(
    near_in,
    dens_block_in,
    dens_dest_in,
    dens_near_in,
    position_in,
    velocity_in,
    mass_in,
    energy_in,
    width_in,
    e_out,
    l_out,
    beside,
    r2_ref,
    mx_ref,
    tot_ref,
    mom_ref,
    slope_ref,
    late,
    own,
    unit,
    near,
    dens_block,
    dens_dest,
    dens_near,
    position,
    velocity,
    mass,
    energy,
    first_width,
    ins,
    ys,
    yr,
    *sems,
):
    half = len(sems) // 2
    early_gather = Gather(own, e_out, True, *sems[:half])
    late_gather = Gather(late, l_out, False, *sems[half:])
    n = lax.axis_index("narrow")

    barrier = pltpu.get_barrier_semaphore()
    partners = [{"narrow": (n + k) % NY} for k in range(1, NY)]
    partners += [early_gather.device(0, 0, 1)]
    partners += [early_gather.device(0, k, 0) for k in range(1, NX)]
    partners += [early_gather.device(d, 0, 0) for d in Z_ORDER[1:] if abs(d) <= RELAY]
    for device in partners:
        pl.semaphore_signal(barrier, inc=1, device_id=device, device_id_type=MESH)

    incoming = [
        pltpu.make_async_copy(src, dst, ins.at[i])
        for i, (src, dst) in enumerate(
            (
                (near_in, near),
                (dens_block_in, dens_block),
                (dens_dest_in, dens_dest),
                (dens_near_in, dens_near),
                (position_in, position),
                (velocity_in, velocity),
                (mass_in, mass),
                (energy_in, energy),
                (width_in, first_width),
            )
        )
    ]
    for copy in incoming:
        copy.start()
    for copy in incoming:
        copy.wait()

    rows = lax.broadcasted_iota(jnp.int32, (NB, BLK), 0)
    for b in range(NB):
        for q in range(3):
            own[b, pl.ds(q, 1)] = position[pl.ds(q, 1), pl.ds(b * BLK, BLK)]
            own[b, pl.ds(3 + q, 1)] = velocity[pl.ds(q, 1), pl.ds(b * BLK, BLK)]
        own[b, pl.ds(6, 1)] = mass[pl.ds(b, 1)]
        own[b, pl.ds(7, 1)] = energy[pl.ds(b, 1)]
        unit[b] = jnp.where(rows == b, 1.0, 0.0)

    def set_slope(width):
        slope = -LOG2E / (width * width)
        for b in range(NB):
            slope_ref[b] = slope[b : b + 1]

    width = first_width[...]
    set_slope(width)

    def local_first(item, carry):
        target = own[item]
        first_sums(
            item,
            target,
            (target, own[near[item]]),
            slope_ref[item],
            r2_ref,
            mx_ref,
            tot_ref,
            mom_ref,
        )
        return carry

    lax.fori_loop(0, NB, local_first, 0)
    beside[pl.ds(pl.multiple_of(n * NB, NB), NB)] = own[...]

    pl.semaphore_wait(barrier, len(partners))

    y_copies = []
    for k in range(1, NY):
        y_copies.append(
            remote(
                own,
                beside.at[pl.ds(pl.multiple_of(n * NB, NB), NB)],
                ys.at[NY - k],
                yr.at[NY - k],
                {"narrow": (n + k) % NY},
            )
        )
        y_copies[-1].start()
    early_gather.start()
    for copy in y_copies:
        copy.wait_recv()

    def export_first(e, carry):
        block = dens_block[e]
        first_sums(
            NB + e,
            own[block],
            tuple(beside[dens_dest[e] * NB + dens_near[s, e]] for s in range(2)),
            slope_ref[block],
            r2_ref,
            mx_ref,
            tot_ref,
            mom_ref,
        )
        return carry

    lax.fori_loop(0, XN, export_first, 0)

    def follow(steps):
        for which, kind, batch in steps:
            gather = early_gather if which == "E" else late_gather
            {"z": gather.z_step, "n": gather.x_near, "f": gather.x_far}[kind](int(batch))

    def combined(ref):
        value = ref[pl.ds(0, NB)]
        for e in range(XN):
            value = value + unit[dens_block[e]] * ref[pl.ds(NB + e, 1)]
        return value

    follow(AFTER_FIRST_PASS)
    for step in range(PASSES):
        if step == PASSES - 1:
            follow(BEFORE_LAST_PASS)
        if step > 0:

            def local_next(item, carry):
                next_sums(item, slope_ref[item], r2_ref, mx_ref, tot_ref, mom_ref)
                return carry

            def export_next(e, carry):
                next_sums(NB + e, slope_ref[dens_block[e]], r2_ref, mx_ref, tot_ref, mom_ref)
                return carry

            lax.fori_loop(0, NB, local_next, 0)
            lax.fori_loop(0, XN, export_next, 0)
        total = combined(tot_ref)
        if step + 1 < PASSES:
            moment = combined(mom_ref)
            ratio = jnp.log(KERNEL_NORM * total / (TARGET_COUNT * mass[...]))
            bend = 2.0 * moment / (width * width * total)
            width = width * jnp.exp(-ratio / (3.0 + bend))
            set_slope(width)

    late[pl.ds(0, NB)] = width
    late[pl.ds(NB, NB)] = KERNEL_NORM * total / (width * width * width)
    late_gather.start()
    follow(AFTER_DENSITY)
    early_gather.finish()
    late_gather.finish()
    for copy in y_copies:
        copy.wait_send()


def gather_call(*args):
    batches = len(BATCHES)
    dma = pltpu.SemaphoreType.DMA
    per_gather = [dma((NZ + 1,)), dma((NZ + 1,))] + [dma((NX, batches))] * 4 + [dma]
    return pl.pallas_call(
        gather_kernel,
        out_shape=(
            jax.ShapeDtypeStruct((NC, NX, NZ, NB, 8, BLK), F32),
            jax.ShapeDtypeStruct((NC, NX, NZ, 2 * NB, BLK), F32),
        ),
        in_specs=[pl.BlockSpec(memory_space=pl.ANY)] * 9,
        out_specs=(pl.BlockSpec(memory_space=pl.ANY),) * 2,
        scratch_shapes=[
            pltpu.VMEM((NY * NB, 8, BLK), F32),
            pltpu.VMEM((NB + XN, 2 * BLK, BLK), F32),
            pltpu.VMEM((NB + XN, 2 * BLK, BLK), F32),
            pltpu.VMEM((NB + XN, BLK), F32),
            pltpu.VMEM((NB + XN, BLK), F32),
            pltpu.VMEM((NB, 1, BLK), F32),
            pltpu.VMEM((2 * NB, BLK), F32),
            pltpu.VMEM((NB, 8, BLK), F32),
            pltpu.VMEM((NB, NB, BLK), F32),
            pltpu.SMEM((NB,), jnp.int32),
            pltpu.SMEM((XN,), jnp.int32),
            pltpu.SMEM((XN,), jnp.int32),
            pltpu.SMEM((2, XN), jnp.int32),
            pltpu.VMEM((3, NB * BLK), F32),
            pltpu.VMEM((3, NB * BLK), F32),
            pltpu.VMEM((NB, BLK), F32),
            pltpu.VMEM((NB, BLK), F32),
            pltpu.VMEM((NB, BLK), F32),
            dma((9,)),
            dma((NY,)),
            dma((NY,)),
        ]
        + per_gather * 2,
        compiler_params=pltpu.CompilerParams(
            collective_id=0, has_side_effects=True, vmem_limit_bytes=62 * 2**20
        ),
        name="density_and_gather",
    )(*args)


def split_two(value):
    high = value.astype(BF16).astype(F32)
    return high, value - high


def split_three(value):
    high, rest = split_two(value)
    return (high,) + split_two(rest)


def target_features(tile, exp_i, scale_i):
    row = lax.broadcasted_iota(jnp.int32, tile.shape, 0)
    swapped = jnp.where(row < 3, pltpu.roll(tile, 5, 0), pltpu.roll(tile, 3, 0))
    squares = jnp.sum(jnp.where(row < 3, tile * tile, 0.0), axis=0, keepdims=True)
    crosses = jnp.sum(jnp.where(row < 3, tile * swapped, 0.0), axis=0, keepdims=True)
    distance = jnp.where(row < 3, -2.0 * tile, jnp.where(row == 6, 1.0, 0.0))
    approach = jnp.where(row < 6, -40.0 * swapped, jnp.where(row == 7, 40.0, 0.0))
    outs = []
    for factor, constant in (
        (distance, squares),
        (approach, 40.0 * crosses),
        (distance * exp_i, squares * exp_i + scale_i),
    ):
        h, m, l = split_three(factor)
        ch, cm, cl = split_three(constant)
        constants = jnp.where(row == 0, ch, jnp.where(row == 1, cm, jnp.where(row == 2, cl, 0.0)))
        full = jnp.concatenate([h, m, l, h, m, h, constants] + [jnp.zeros_like(h)] * 9, axis=0)
        outs.append(full.T)
    return jnp.concatenate(outs, axis=0).astype(BF16)[:, :KF]


T_SQ, T_CROSS, T_EXP, T_SCALE, T_WIDTH, T_SOUND, T_RHO, T_PRESS = range(8)


def slot_table(tab_ref, slot, tiles_ref, late_ref):
    def column(q):
        return tiles_ref[slot, pl.ds(q, NB, stride=8)]

    x, y, z, vx, vy, vz = (column(q) for q in range(6))
    energy = column(7)
    width = late_ref[slot, pl.ds(0, NB)]
    rho = late_ref[slot, pl.ds(NB, NB)]
    tab_ref[slot, T_SQ] = x * x + y * y + z * z
    tab_ref[slot, T_CROSS] = x * vx + y * vy + z * vz
    tab_ref[slot, T_EXP] = -LOG2E / (width * width)
    tab_ref[slot, T_SCALE] = math.log2(2.0 * KERNEL_NORM) - 5.0 * jnp.log2(width)
    tab_ref[slot, T_WIDTH] = 0.05 * width
    tab_ref[slot, T_SOUND] = jnp.sqrt((10.0 / 9.0) * energy)
    tab_ref[slot, T_RHO] = 8.0 * rho
    tab_ref[slot, T_PRESS] = (2.0 / 3.0) * energy / rho


TARGET_VALUES = (T_WIDTH, T_SOUND, T_RHO, T_PRESS)


def force_kernel(
    near_in,
    force_block_in,
    force_dest_in,
    force_near_in,
    tiles_in,
    late_in,
    rho_out,
    acc_out,
    heat_out,
    tab_ref,
    tiles_ref,
    late_ref,
    tl_ref,
    tg_ref,
    acc_ref,
    r0,
    r1,
    f0,
    f1,
    w0,
    w1,
    f2,
    near,
    force_block,
    force_dest,
    force_near,
    lists_v,
    lists,
    ins,
    tile_sems,
    late_sems,
):
    chunk = tiles_ref.shape[0] // CHUNKS
    incoming = [
        pltpu.make_async_copy(src, dst, ins.at[i])
        for i, (src, dst) in enumerate(
            (
                (near_in, near),
                (force_block_in, force_block),
                (force_dest_in, force_dest),
                (force_near_in, force_near),
            )
        )
    ]
    for copy in incoming:
        copy.start()

    loads = []
    for k in range(CHUNKS):
        part = pl.ds(k * chunk, chunk)
        loads.append(
            (
                pltpu.make_async_copy(tiles_in.at[part], tiles_ref.at[part], tile_sems.at[k]),
                pltpu.make_async_copy(late_in.at[part], late_ref.at[part], late_sems.at[k]),
            )
        )
        for copy in loads[-1]:
            copy.start()

    w = lax.axis_index("wide")
    for copy in incoming:
        copy.wait()
    there = force_dest[...]
    dz = ((there >> 3) - (w >> 3)) & 15
    dn = NZ - dz
    spot = jnp.where(
        dz <= NZ // 2,
        jnp.where(dz <= RELAY, 2 * dz + 1, 2 * dz - 1),
        jnp.where(dn <= RELAY, 2 * dn + 2, 2 * dn),
    )
    spot = jnp.where(dz == 0, 0, jnp.where(dz == RELAY, 1, jnp.where(dn == RELAY, 2, spot)))
    slot = (((there ^ w) & 1) * NX + (((there >> 1) - (w >> 1)) & 3)) * NZ + spot
    lists_v[:, pl.ds(0, XW)] = jnp.concatenate(
        [force_block[...], slot * NB + force_near[...]], axis=0
    )
    lists_v[:, pl.ds(XW, XW)] = jnp.zeros((3, XW), jnp.int32)
    to_scalars = pltpu.make_async_copy(lists_v, lists, ins.at[4])
    to_scalars.start()

    def fill(slot, carry):
        slot_table(tab_ref, slot, tiles_ref, late_ref)
        return carry

    def fill_chunk(k):
        for copy in loads[k]:
            copy.wait()
        lax.fori_loop(k * chunk, (k + 1) * chunk, fill, 0, unroll=4)

    fill_chunk(0)

    def prepare(b, carry):
        tl_ref[b] = target_features(
            tiles_ref[0, pl.ds(pl.multiple_of(b * 8, 8), 8)],
            tab_ref[0, T_EXP, pl.ds(b, 1)],
            tab_ref[0, T_SCALE, pl.ds(b, 1)],
        )
        for i, q in enumerate(TARGET_VALUES):
            tg_ref[b, i] = jnp.broadcast_to(tab_ref[0, q, pl.ds(b, 1)], (BLK, BLK)).T
        acc_ref[b] = jnp.zeros((16, 3 * BLK), F32)
        return carry

    lax.fori_loop(0, NB, prepare, 0)
    for k in range(1, CHUNKS):
        fill_chunk(k)
    to_scalars.wait()
    for b in range(NB):
        lists[0, XW + b] = b
        lists[1, XW + b] = b
        lists[2, XW + b] = near[b]
    f1[...] = jnp.zeros(f1.shape, BF16)
    w1[...] = jnp.zeros(w1.shape, BF16)

    def pick(i, q):
        a, b = lists[1, i], lists[2, i]
        return jnp.concatenate(
            [tab_ref[a >> 3, q, pl.ds(a & 7, 1)], tab_ref[b >> 3, q, pl.ds(b & 7, 1)]], axis=1
        )

    def products(i, r_ref, f_ref):
        a, b = lists[1, i], lists[2, i]
        raw = jnp.concatenate(
            [
                tiles_ref[s >> 3, pl.ds(pl.multiple_of((s & 7) * 8, 8), 8)]
                for s in (a, b)
            ],
            axis=1,
        )
        row = lax.broadcasted_iota(jnp.int32, raw.shape, 0)
        cross = pick(i, T_CROSS)
        u = jnp.where(row < 6, raw, jnp.where(row == 6, pick(i, T_SQ), cross))
        h, m, l = split_three(u)
        feats = jnp.concatenate([h, h, h, m, m, l, jnp.ones_like(h), jnp.zeros_like(h)], axis=0)
        r_ref[...] = jnp.dot(tl_ref[lists[0, i]], feats.astype(BF16), preferred_element_type=F32)
        f = jnp.where(row == 6, 1.0, u) * raw[6:7]
        f_ref[...] = jnp.concatenate(split_two(f), axis=0).astype(BF16)

    def pairs(i, r_ref, w_ref):
        b = lists[0, i]
        width_j, sound_j, rho_j, press_j = (pick(i, q) for q in TARGET_VALUES)
        exp_j, scale_j = pick(i, T_EXP), pick(i, T_SCALE)
        for g in range(8):
            r2 = r_ref[pl.ds(16 * g, 16)]
            vd = r_ref[pl.ds(BLK + 16 * g, 16)]

            def own(q):
                value = tg_ref[b, q, pl.ds(16 * g, 16)]
                return jnp.concatenate([value, value], axis=1)

            hs = own(0) + width_j
            nu = jnp.minimum(hs * vd * pl.reciprocal(r2 + hs * hs, approx=True), 0.0)
            visc = nu * (nu - (own(1) + sound_j)) * pl.reciprocal(own(2) + rho_j, approx=True)
            grad_i = jnp.exp2(r_ref[pl.ds(2 * BLK + 16 * g, 16)])
            grad_j = jnp.exp2(r2 * exp_j + scale_j)
            first = own(3) * grad_i
            both = first + visc * (grad_i + grad_j)
            w_ref[pl.ds(16 * g, 16)] = both.astype(BF16)
            w_ref[pl.ds(BLK + 16 * g, 16)] = first.astype(BF16)
            w_ref[pl.ds(2 * BLK + 16 * g, 16)] = (press_j * grad_j).astype(BF16)

    def reduce(i, f_ref, w_ref):
        b = lists[0, i]
        acc_ref[b] = acc_ref[b] + lax.dot_general(
            f_ref[...], w_ref[...], (((1,), (1,)), ((), ())), preferred_element_type=F32
        )

    products(0, r0, f0)

    def body(k, carry):
        i = 2 * k
        reduce(jnp.maximum(i - 1, 0), f1, w1)
        products(i + 1, r1, f1)
        pairs(i, r0, w0)
        products(jnp.minimum(i + 2, ITEMS - 1), r0, f2)
        reduce(i, f0, w0)
        f0[...] = f2[...]
        pairs(i + 1, r1, w1)
        return carry

    lax.fori_loop(0, ITEMS // 2, body, 0, unroll=17)
    reduce(ITEMS - 1, f1, w1)

    rho_out[...] = late_ref[0, pl.ds(NB, NB)]
    for b in range(NB):
        tile = tiles_ref[0, pl.ds(8 * b, 8)]
        s = acc_ref[b]
        s = s[0:8] + s[8:16]
        push, heat = s[:, 0:BLK] + s[:, 2 * BLK :], s[:, 0:BLK] + s[:, BLK : 2 * BLK]
        for q in range(3):
            acc_out[pl.ds(q, 1), pl.ds(b * BLK, BLK)] = tile[q : q + 1] * push[6:7] - push[q : q + 1]
        value = tab_ref[0, T_CROSS, pl.ds(b, 1)] * heat[6:7] + heat[7:8]
        for q in range(3):
            value = value - tile[3 + q : 4 + q] * heat[q : q + 1]
            value = value - tile[q : q + 1] * heat[3 + q : 4 + q]
        heat_out[pl.ds(b, 1)] = -0.5 * value


def force_call(*args):
    vmem = pl.BlockSpec(memory_space=pltpu.VMEM)
    slots = NC * NX * NZ
    return pl.pallas_call(
        force_kernel,
        out_shape=(
            jax.ShapeDtypeStruct((NB, BLK), F32),
            jax.ShapeDtypeStruct((3, NB * BLK), F32),
            jax.ShapeDtypeStruct((NB, BLK), F32),
        ),
        in_specs=[pl.BlockSpec(memory_space=pl.ANY)] * 6,
        out_specs=(vmem,) * 3,
        scratch_shapes=[
            pltpu.VMEM((slots, 8, NB, BLK), F32),
            pltpu.VMEM((slots, 8 * NB, BLK), F32),
            pltpu.VMEM((slots, 2 * NB, BLK), F32),
            pltpu.VMEM((NB, 3 * BLK, KF), BF16),
            pltpu.VMEM((NB, len(TARGET_VALUES), BLK, BLK), F32),
            pltpu.VMEM((NB, 16, 3 * BLK), F32),
            pltpu.VMEM((3 * BLK, 2 * BLK), F32),
            pltpu.VMEM((3 * BLK, 2 * BLK), F32),
            pltpu.VMEM((16, 2 * BLK), BF16),
            pltpu.VMEM((16, 2 * BLK), BF16),
            pltpu.VMEM((3 * BLK, 2 * BLK), BF16),
            pltpu.VMEM((3 * BLK, 2 * BLK), BF16),
            pltpu.VMEM((16, 2 * BLK), BF16),
            pltpu.SMEM((NB,), jnp.int32),
            pltpu.VMEM((1, XW), jnp.int32),
            pltpu.VMEM((1, XW), jnp.int32),
            pltpu.VMEM((2, XW), jnp.int32),
            pltpu.VMEM((3, 2 * XW), jnp.int32),
            pltpu.SMEM((3, 2 * XW), jnp.int32),
            pltpu.SemaphoreType.DMA((5,)),
            pltpu.SemaphoreType.DMA((CHUNKS,)),
            pltpu.SemaphoreType.DMA((CHUNKS,)),
        ],
        compiler_params=pltpu.CompilerParams(vmem_limit_bytes=62 * 2**20),
        name="force",
    )(*args)


def on_device(
    position,
    velocity,
    mass,
    energy,
    smoothing,
    local_near,
    dens_block,
    dens_dest,
    dens_near,
    force_block,
    force_dest,
    force_near,
):
    tiles, late = gather_call(
        local_near,
        dens_block,
        dens_dest.reshape(-1),
        dens_near.T,
        position,
        velocity,
        mass.reshape(NB, BLK),
        energy.reshape(NB, BLK),
        smoothing.reshape(NB, BLK),
    )
    slots = NC * NX * NZ
    rho, accel, heat = force_call(
        local_near,
        force_block.reshape(1, XW),
        force_dest.T,
        force_near.T,
        tiles.reshape(slots, 8 * NB, BLK),
        late.reshape(slots, 2 * NB, BLK),
    )
    return rho.reshape(NB * BLK), accel, heat.reshape(NB * BLK)


def solution(mesh):
    both = ("wide", "narrow")
    in_specs = (
        P(None, both),
        P(None, both),
        P(both),
        P(both),
        P(both),
        P(both),
        P(both),
        P(both, None),
        P(both, None),
        P(both),
        P(both, None),
        P(both, None),
    )
    out_specs = (P(both), P(None, both), P(both))
    return jax.shard_map(
        on_device, mesh=mesh, in_specs=in_specs, out_specs=out_specs, check_vma=False
    )
```

time: 96.1 us -> 72.9 us (0.76)
  Pallas kernels: 86.6 us -> 72.1 us
  other arithmetic: 5.01 us -> 0 us
  local copies, waits for them, and re-layouts: 3.53 us -> 0 us
    pallas_call x1, Pallas kernels: 58.8 us -> 49.3 us  [gather_call(): pl.pallas_call(gather_kernel, out_shape=(jax.ShapeDtypeStruct((NC, NX, NZ...]
    pallas_call x1, Pallas kernels: 27.8 us -> 22.8 us  [force_call(): pl.pallas_call(force_kernel, out_shape=(jax.ShapeDtypeStruct((NB, BLK), F...]
    unnamed x9 -> x0, local copies, waits for them, and re-layouts: 3.29 us -> none
    add x4 -> x0, other arithmetic: 2.75 us -> none  [the longest x2 1.35 us: on_device(): row * NB + dens_near]
where the time goes in v2:
time: 72.9 us; the launch traced here: 72.8 us
  Pallas kernels  72.1 us (99%)
    pallas_call x1, Pallas kernels, gather_call(): pl.pallas_call(gather_kernel, out_shape=(jax.ShapeDtypeStruct((NC, NX, NZ...  49.3 us
    pallas_call x1, Pallas kernels, force_call(): pl.pallas_call(force_kernel, out_shape=(jax.ShapeDtypeStruct((NB, BLK), F...  22.8 us

profile of v2, /device:TPU:1, one launch (start us, length us, event | category | flops | bytes accessed | tf_op | source)
XLA Modules:
  0.0 72.8 jit_solution(4395143919923850825)
XLA Ops:
  0.6 49.3 %density_and_gather.1 = (f32[2,4,16,8,8,128]{5,4,3,2,1,0:T(8,128)}, f32[2,4,16,16,128]{4,3,2,1,0:T(8,128)}) custom-call(s32[8]{0:T(128)} %near_in.3, s32[8]{0:T(128)} %dens_block_in.1, s32[8]{0:T(128)} %bitcast.19, s32[2,8]{1,0:T(2,128)} %bitcast.18, f32[3,1024]{1,0:T(4,128)} %position_in.1, f32[3,1024]{1,0:T(4,128)} %velocity_in.1, f32[8,128]{1,0:T(8,128)} %bitcast.14, ...), custom_call_target="tpu_custom_call" | custom-call | tf_op jit(solution)/shard_map/density_and_gather/pallas_call | solution.py:397
  49.9 22.8 %force.1 = (f32[8,128]{1,0:T(8,128)}, f32[3,1024]{1,0:T(4,128)}, f32[8,128]{1,0:T(8,128)}) custom-call(s32[8]{0:T(128)} %near_in.3, s32[1,128]{1,0:T(1,128)} %bitcast.20, s32[1,128]{1,0:T(1,128)} %bitcast.21, s32[2,128]{1,0:T(2,128)} %bitcast.17, f32[128,64,128]{2,1,0:T(8,128)} %bitcast.12, f32[128,16,128]{2,1,0:T(8,128)} %bitcast.13), custom_call_target="tpu_custom_call" | custom-call | tf_op jit(solution)/shard_map/force/pallas_call | solution.py:691

commit v3 on v2

--- a/solution.py
+++ b/solution.py
@@ -51,6 +51,10 @@
     "Ef3", "Ln1", "Lf1", "Ef4", "Ln2", "Lf2", "Ln3", "Lf3",
     "Ln4", "Lf4",
 )
+
+
+UNROLL_FIRST = 4
+UNROLL_NEXT = 8
 
 
 class Gather:
@@ -308,7 +312,7 @@
         )
         return carry
 
-    lax.fori_loop(0, NB, local_first, 0)
+    lax.fori_loop(0, NB, local_first, 0, unroll=UNROLL_FIRST)
     beside[pl.ds(pl.multiple_of(n * NB, NB), NB)] = own[...]
 
     pl.semaphore_wait(barrier, len(partners))
@@ -343,7 +347,7 @@
         )
         return carry
 
-    lax.fori_loop(0, XN, export_first, 0)
+    lax.fori_loop(0, XN, export_first, 0, unroll=UNROLL_FIRST)
 
     def follow(steps):
         for which, kind, batch in steps:
@@ -370,8 +374,8 @@
                 next_sums(NB + e, slope_ref[dens_block[e]], r2_ref, mx_ref, tot_ref, mom_ref)
                 return carry
 
-            lax.fori_loop(0, NB, local_next, 0)
-            lax.fori_loop(0, XN, export_next, 0)
+            lax.fori_loop(0, NB, local_next, 0, unroll=UNROLL_NEXT)
+            lax.fori_loop(0, XN, export_next, 0, unroll=UNROLL_NEXT)
         total = combined(tot_ref)
         if step + 1 < PASSES:
             moment = combined(mom_ref)
@@ -545,9 +549,12 @@
                 pltpu.make_async_copy(late_in.at[part], late_ref.at[part], late_sems.at[k]),
             )
         )
-        for copy in loads[-1]:
+
+    def start_load(k):
+        for copy in loads[k]:
             copy.start()
 
+    start_load(0)
     w = lax.axis_index("wide")
     for copy in incoming:
         copy.wait()
@@ -567,6 +574,8 @@
     lists_v[:, pl.ds(XW, XW)] = jnp.zeros((3, XW), jnp.int32)
     to_scalars = pltpu.make_async_copy(lists_v, lists, ins.at[4])
     to_scalars.start()
+    for k in range(1, CHUNKS):
+        start_load(k)
 
     def fill(slot, carry):
         slot_table(tab_ref, slot, tiles_ref, late_ref)
@@ -590,7 +599,7 @@
         acc_ref[b] = jnp.zeros((16, 3 * BLK), F32)
         return carry
 
-    lax.fori_loop(0, NB, prepare, 0)
+    lax.fori_loop(0, NB, prepare, 0, unroll=4)
     for k in range(1, CHUNKS):
         fill_chunk(k)
     to_scalars.wait()

time: 72.9 us -> 70.8 us (0.971)
  Pallas kernels: 72.1 us -> 70 us
    pallas_call x1, Pallas kernels: 22.8 us -> 21.3 us  [force_call(): pl.pallas_call(force_kernel, out_shape=(jax.ShapeDtypeStruct((NB, BLK), F...]
where the time goes in v3:
time: 70.8 us; the launch traced here: 70.6 us
  Pallas kernels  70 us (99%)
    pallas_call x1, Pallas kernels, gather_call(): pl.pallas_call(gather_kernel, out_shape=(jax.ShapeDtypeStruct((NC, NX, NZ...  48.6 us
    pallas_call x1, Pallas kernels, force_call(): pl.pallas_call(force_kernel, out_shape=(jax.ShapeDtypeStruct((NB, BLK), F...  21.3 us

profile of v3, /device:TPU:1, one launch (start us, length us, event | category | flops | bytes accessed | tf_op | source)
XLA Modules:
  0.0 70.6 jit_solution(1515838350540226219)
XLA Ops:
  0.6 48.6 %density_and_gather.1 = (f32[2,4,16,8,8,128]{5,4,3,2,1,0:T(8,128)}, f32[2,4,16,16,128]{4,3,2,1,0:T(8,128)}) custom-call(s32[8]{0:T(128)} %near_in.3, s32[8]{0:T(128)} %dens_block_in.1, s32[8]{0:T(128)} %bitcast.19, s32[2,8]{1,0:T(2,128)} %bitcast.18, f32[3,1024]{1,0:T(4,128)} %position_in.1, f32[3,1024]{1,0:T(4,128)} %velocity_in.1, f32[8,128]{1,0:T(8,128)} %bitcast.14, ...), custom_call_target="tpu_custom_call" | custom-call | tf_op jit(solution)/shard_map/density_and_gather/pallas_call | solution.py:401
  49.2 21.3 %force.1 = (f32[8,128]{1,0:T(8,128)}, f32[3,1024]{1,0:T(4,128)}, f32[8,128]{1,0:T(8,128)}) custom-call(s32[8]{0:T(128)} %near_in.3, s32[1,128]{1,0:T(1,128)} %bitcast.20, s32[1,128]{1,0:T(1,128)} %bitcast.21, s32[2,128]{1,0:T(2,128)} %bitcast.17, f32[128,64,128]{2,1,0:T(8,128)} %bitcast.12, f32[128,16,128]{2,1,0:T(8,128)} %bitcast.13), custom_call_target="tpu_custom_call" | custom-call | tf_op jit(solution)/shard_map/force/pallas_call | solution.py:700

commit v4 on v3

--- a/solution.py
+++ b/solution.py
@@ -489,7 +489,7 @@
     tab_ref[slot, T_PRESS] = (2.0 / 3.0) * energy / rho
 
 
-TARGET_VALUES = (T_WIDTH, T_SOUND, T_RHO, T_PRESS)
+TARGET_VALUES = (T_WIDTH, T_SOUND, T_RHO)
 
 
 def force_kernel(
@@ -632,11 +632,12 @@
         feats = jnp.concatenate([h, h, h, m, m, l, jnp.ones_like(h), jnp.zeros_like(h)], axis=0)
         r_ref[...] = jnp.dot(tl_ref[lists[0, i]], feats.astype(BF16), preferred_element_type=F32)
         f = jnp.where(row == 6, 1.0, u) * raw[6:7]
-        f_ref[...] = jnp.concatenate(split_two(f), axis=0).astype(BF16)
+        pressed = f * pick(i, T_PRESS)
+        f_ref[...] = jnp.concatenate(split_two(f) + split_two(pressed), axis=0).astype(BF16)
 
     def pairs(i, r_ref, w_ref):
         b = lists[0, i]
-        width_j, sound_j, rho_j, press_j = (pick(i, q) for q in TARGET_VALUES)
+        width_j, sound_j, rho_j = (pick(i, q) for q in TARGET_VALUES)
         exp_j, scale_j = pick(i, T_EXP), pick(i, T_SCALE)
         for g in range(8):
             r2 = r_ref[pl.ds(16 * g, 16)]
@@ -651,17 +652,19 @@
             visc = nu * (nu - (own(1) + sound_j)) * pl.reciprocal(own(2) + rho_j, approx=True)
             grad_i = jnp.exp2(r_ref[pl.ds(2 * BLK + 16 * g, 16)])
             grad_j = jnp.exp2(r2 * exp_j + scale_j)
-            first = own(3) * grad_i
-            both = first + visc * (grad_i + grad_j)
-            w_ref[pl.ds(16 * g, 16)] = both.astype(BF16)
-            w_ref[pl.ds(BLK + 16 * g, 16)] = first.astype(BF16)
-            w_ref[pl.ds(2 * BLK + 16 * g, 16)] = (press_j * grad_j).astype(BF16)
+            w_ref[pl.ds(16 * g, 16)] = (visc * (grad_i + grad_j)).astype(BF16)
+            w_ref[pl.ds(BLK + 16 * g, 16)] = grad_i.astype(BF16)
+            w_ref[pl.ds(2 * BLK + 16 * g, 16)] = grad_j.astype(BF16)
 
     def reduce(i, f_ref, w_ref):
         b = lists[0, i]
-        acc_ref[b] = acc_ref[b] + lax.dot_general(
-            f_ref[...], w_ref[...], (((1,), (1,)), ((), ())), preferred_element_type=F32
-        )
+        for rows, cols in ((0, pl.ds(0, 2 * BLK)), (16, pl.ds(2 * BLK, BLK))):
+            acc_ref[b, :, cols] = acc_ref[b, :, cols] + lax.dot_general(
+                f_ref[pl.ds(rows, 16)],
+                w_ref[cols],
+                (((1,), (1,)), ((), ())),
+                preferred_element_type=F32,
+            )
 
     products(0, r0, f0)
 
@@ -676,7 +679,7 @@
         pairs(i + 1, r1, w1)
         return carry
 
-    lax.fori_loop(0, ITEMS // 2, body, 0, unroll=17)
+    lax.fori_loop(0, ITEMS // 2, body, 0, unroll=34)
     reduce(ITEMS - 1, f1, w1)
 
     rho_out[...] = late_ref[0, pl.ds(NB, NB)]
@@ -684,7 +687,8 @@
         tile = tiles_ref[0, pl.ds(8 * b, 8)]
         s = acc_ref[b]
         s = s[0:8] + s[8:16]
-        push, heat = s[:, 0:BLK] + s[:, 2 * BLK :], s[:, 0:BLK] + s[:, BLK : 2 * BLK]
+        visc, first = s[:, 0:BLK], tab_ref[0, T_PRESS, pl.ds(b, 1)] * s[:, BLK : 2 * BLK]
+        push, heat = first + visc + s[:, 2 * BLK :], 2.0 * first + visc
         for q in range(3):
             acc_out[pl.ds(q, 1), pl.ds(b * BLK, BLK)] = tile[q : q + 1] * push[6:7] - push[q : q + 1]
         value = tab_ref[0, T_CROSS, pl.ds(b, 1)] * heat[6:7] + heat[7:8]
@@ -715,11 +719,11 @@
             pltpu.VMEM((NB, 16, 3 * BLK), F32),
             pltpu.VMEM((3 * BLK, 2 * BLK), F32),
             pltpu.VMEM((3 * BLK, 2 * BLK), F32),
-            pltpu.VMEM((16, 2 * BLK), BF16),
-            pltpu.VMEM((16, 2 * BLK), BF16),
+            pltpu.VMEM((32, 2 * BLK), BF16),
+            pltpu.VMEM((32, 2 * BLK), BF16),
             pltpu.VMEM((3 * BLK, 2 * BLK), BF16),
             pltpu.VMEM((3 * BLK, 2 * BLK), BF16),
-            pltpu.VMEM((16, 2 * BLK), BF16),
+            pltpu.VMEM((32, 2 * BLK), BF16),
             pltpu.SMEM((NB,), jnp.int32),
             pltpu.VMEM((1, XW), jnp.int32),
             pltpu.VMEM((1, XW), jnp.int32),

time: 70.8 us -> 70.1 us (level)
  Pallas kernels: 70 us -> 69.1 us
    pallas_call x1, Pallas kernels: 21.3 us -> 20.5 us  [force_call(): pl.pallas_call(force_kernel, out_shape=(jax.ShapeDtypeStruct((NB, BLK), F...]
where the time goes in v4:
time: 70.1 us; the launch traced here: 69.9 us
  Pallas kernels  69.1 us (99%)
  between operations  0.8 us (1%)
    pallas_call x1, Pallas kernels, gather_call(): pl.pallas_call(gather_kernel, out_shape=(jax.ShapeDtypeStruct((NC, NX, NZ...  48.6 us
    pallas_call x1, Pallas kernels, force_call(): pl.pallas_call(force_kernel, out_shape=(jax.ShapeDtypeStruct((NB, BLK), F...  20.5 us

profile of v4, /device:TPU:1, one launch (start us, length us, event | category | flops | bytes accessed | tf_op | source)
XLA Modules:
  0.0 69.9 jit_solution(12419879044465101285)
XLA Ops:
  0.6 48.6 %density_and_gather.1 = (f32[2,4,16,8,8,128]{5,4,3,2,1,0:T(8,128)}, f32[2,4,16,16,128]{4,3,2,1,0:T(8,128)}) custom-call(s32[8]{0:T(128)} %near_in.3, s32[8]{0:T(128)} %dens_block_in.1, s32[8]{0:T(128)} %bitcast.19, s32[2,8]{1,0:T(2,128)} %bitcast.18, f32[3,1024]{1,0:T(4,128)} %position_in.1, f32[3,1024]{1,0:T(4,128)} %velocity_in.1, f32[8,128]{1,0:T(8,128)} %bitcast.14, ...), custom_call_target="tpu_custom_call" | custom-call | tf_op jit(solution)/shard_map/density_and_gather/pallas_call | solution.py:401
  49.2 20.5 %force.1 = (f32[8,128]{1,0:T(8,128)}, f32[3,1024]{1,0:T(4,128)}, f32[8,128]{1,0:T(8,128)}) custom-call(s32[8]{0:T(128)} %near_in.3, s32[1,128]{1,0:T(1,128)} %bitcast.20, s32[1,128]{1,0:T(1,128)} %bitcast.21, s32[2,128]{1,0:T(2,128)} %bitcast.17, f32[128,64,128]{2,1,0:T(8,128)} %bitcast.12, f32[128,16,128]{2,1,0:T(8,128)} %bitcast.13), custom_call_target="tpu_custom_call" | custom-call | tf_op jit(solution)/shard_map/force/pallas_call | solution.py:704
